TPU v7x, 32 devices: a whole 2x2x4 slice. The times are simulated.
32 devices in a mesh: clip: 8 (over y, x, core), sp: 4 (over z).
Axes of the slice: x: 2, y: 2, z: 4, core: 2. Of those that a mesh axis runs over, the one named last changes fastest.
Arguments:
- queries: bfloat16 [4096, 6144], P(('clip', 'sp')), parts along dimension 0, may hold values from -256 to 256
- key_codes: bfloat16 [4096, 1024], P(('clip', 'sp')), parts along dimension 0, may hold values from -7 to 7
- value_codes: bfloat16 [4096, 1024], P(('clip', 'sp')), parts along dimension 0, may hold values from -6 to 6
- key_scales: bfloat16 [32, 8], P(('clip', 'sp')), parts along dimension 0, may hold values from 0.25 to 2
- value_scales: bfloat16 [32, 8], P(('clip', 'sp')), parts along dimension 0, may hold values from 0.25 to 2
- masks: int32 [384, 4, 4], P('clip'), parts along dimension 0, may hold values from 0 to 1, as said below
Outputs:
- attended: bfloat16 [4096, 6144], P(('clip', 'sp')), parts along dimension 0
There are 8 independent parts, one for each index of `clip`. A program takes and returns all parts, laid end to end along the dimension named above; each array names one. Nothing has to cross between parts.
Inputs may be any that keep to these rules, and one draw needn't show every extreme that they name: masks[h, a, b] is 1 where query tile a of head h attends to key tile b and 0 where it does not; every diagonal tile (a == b) is 1; the share of kept tiles differs from head to head.
All inputs are finite; a program needn't handle non-finite values.
Results may differ from a plain program's by a relative error of at most 0.0038.
Values may be sent and summed in bfloat16 or wider, within the bound.
A program may use at most 128 MiB of HBM per device.

v0:
```python
import math

import jax
import jax.numpy as jnp
from jax import lax
from jax.sharding import PartitionSpec as P

QH = 48
KVH = 8
HD = 128
TILE = 128


NEGATIVE = -1e30


def local(queries, key_codes, value_codes, key_scales, value_scales, masks):
    tok_count = queries.shape[0]
    per_group = QH // KVH
    query_tiles = tok_count // TILE
    inverse = 1.0 / math.sqrt(HD)
    grouped = queries.reshape(tok_count, KVH, per_group, HD)
    tile_rows = key_scales.shape[0]
    key_tokens = jnp.broadcast_to(key_scales[:, None, :], (tile_rows, TILE, KVH)).reshape(
        tok_count, KVH
    )
    value_tokens = jnp.broadcast_to(value_scales[:, None, :], (tile_rows, TILE, KVH)).reshape(
        tok_count, KVH
    )
    tile_count = masks.shape[1]
    my_mask = lax.dynamic_slice_in_dim(masks, lax.axis_index("sp") * query_tiles, query_tiles, 1)
    my_mask = my_mask.reshape(KVH, per_group, query_tiles, tile_count)
    initial = (
        jnp.full((KVH, per_group, tok_count), NEGATIVE, jnp.float32),
        jnp.zeros((KVH, per_group, tok_count), jnp.float32),
        jnp.zeros((tok_count, KVH, per_group, HD), jnp.float32),
    )
    key_heads = key_codes.reshape(tok_count, KVH, HD)
    value_heads = value_codes.reshape(tok_count, KVH, HD)
    carry = initial
    key_piece = lax.all_gather(key_heads, "sp", axis=0, tiled=True)
    value_piece = lax.all_gather(value_heads, "sp", axis=0, tiled=True)
    key_piece_scale = lax.all_gather(key_tokens, "sp", axis=0, tiled=True)
    value_piece_scale = lax.all_gather(value_tokens, "sp", axis=0, tiled=True)
    key_count = key_piece.shape[0]
    key_block = math.gcd(key_count, 512)
    block_count = key_count // key_block
    block_tiles = key_block // TILE

    def inner(state, operands):
        running_max, totals, running = state
        key_part, value_part, key_scale, value_scale, position = operands
        first = position * key_block
        scores = jnp.einsum("rkgd,jkd->kgrj", grouped, key_part, preferred_element_type=jnp.float32)
        scores = scores * (key_scale.astype(jnp.float32).T * inverse)[:, None, None, :]
        scores = scores.reshape(KVH, per_group, query_tiles, TILE, block_tiles, TILE)
        columns = lax.dynamic_slice_in_dim(my_mask, first // TILE, block_tiles, 3)
        keep = (columns > 0)[:, :, :, None, :, None]
        scores = jnp.where(keep, scores, NEGATIVE)
        new_max = jnp.maximum(
            running_max, jnp.max(scores, axis=(4, 5)).reshape(KVH, per_group, tok_count)
        )
        rescale = jnp.exp(running_max - new_max)
        expo = jnp.where(
            keep, jnp.exp(scores - new_max.reshape(KVH, per_group, query_tiles, TILE, 1, 1)), 0.0
        )
        totals = totals * rescale + jnp.sum(expo, axis=(4, 5)).reshape(KVH, per_group, tok_count)
        factor = value_scale.astype(jnp.float32).T.reshape(KVH, 1, 1, 1, block_tiles, TILE)
        weighted = (
            (expo * factor).astype(jnp.bfloat16).reshape(KVH, per_group, tok_count, key_block)
        )
        added = jnp.einsum(
            "kgrj,jkd->rkgd", weighted, value_part, preferred_element_type=jnp.float32
        )
        running = running * jnp.transpose(rescale, (2, 0, 1))[..., None] + added
        return ((new_max, totals, running), None)

    operands = (
        key_piece.reshape(block_count, key_block, KVH, HD),
        value_piece.reshape(block_count, key_block, KVH, HD),
        key_piece_scale.reshape(block_count, key_block, KVH),
        value_piece_scale.reshape(block_count, key_block, KVH),
        jnp.arange(block_count, dtype=jnp.int32),
    )
    carry, unused = lax.scan(inner, carry, operands)
    final_max, totals, running = carry
    normed = running / jnp.transpose(totals, (2, 0, 1))[..., None]
    return normed.astype(jnp.bfloat16).reshape(tok_count, QH * HD)


def solution(mesh):
    in_specs = (
        P(("clip", "sp"), None),
        P(("clip", "sp"), None),
        P(("clip", "sp"), None),
        P(("clip", "sp"), None),
        P(("clip", "sp"), None),
        P("clip", None, None),
    )
    out_specs = P(("clip", "sp"), None)
    return jax.shard_map(local, mesh=mesh, in_specs=in_specs, out_specs=out_specs, check_vma=False)
```

profile of v0, /device:TPU:0, one launch (start us, length us, event | category | flops | bytes accessed | tf_op | source)
XLA Modules:
  0.0 89.9 jit_solution(12978026286349056272)
XLA Ops:
  6.5 0.0 all-gather.3.cloned.1.call-start
  6.5 1.1 %copy.14 = bf16[128,1024]{0,1:T(8,128)(2,1)S(1)} copy(bf16[128,1024]{1,0:T(8,128)(2,1)} %param.7) | data formatting | bytes 524288 | tf_op args[1]
  7.7 0.9 copy.15
  8.5 0.0 all-gather.3.cloned.1.call-update
  8.5 0.0 all-gather.5.cloned.1.call-start
  8.6 1.8 %copy.18 = bf16[128,1024]{0,1:T(8,128)(2,1)} copy(bf16[128,1024]{1,0:T(8,128)(2,1)} %param.8) | data formatting | bytes 524288 | tf_op args[2]
  10.4 0.0 all-gather.5.cloned.1.call-update
  10.4 0.7 dynamic-slice_compare_fusion
  11.1 0.1 gt.14
  11.2 0.1 copy.12
  11.3 0.1 broadcast_bitcast_fusion
  11.4 0.7 reshape.97
  12.2 13.6 %all_gather.13 = bf16[512,8]{0,1:T(8,128)(2,1)S(1)} all-gather(bf16[128,8]{0,1:T(8,128)(2,1)S(1)} %reshape.97), channel_id=1, replica_groups=mesh['clip'=8,'sp'=4] {'sp'}, dimensions={0}, use_global_device_ids=true | all-gather | bytes 10240 | tf_op jit(solution)/shard_map/all_gather | solution.py:43
  25.8 1.9 %copy.16 = bf16[128,6144]{0,1:T(8,128)(2,1)S(1)} copy(bf16[128,6144]{1,0:T(8,128)(2,1)} %param.6) | data formatting | bytes 3145728 | tf_op args[0]
  27.7 0.7 reshape.98
  28.5 12.0 %all_gather.14 = bf16[512,8]{0,1:T(8,128)(2,1)S(1)} all-gather(bf16[128,8]{0,1:T(8,128)(2,1)S(1)} %reshape.98), channel_id=1, replica_groups=mesh['clip'=8,'sp'=4] {'sp'}, dimensions={0}, use_global_device_ids=true | all-gather | bytes 10240 | tf_op jit(solution)/shard_map/all_gather | solution.py:44
  40.4 0.0 all-gather.3.cloned.1.call-done
  40.4 6.7 %fusion = (f32[8,6,128]{2,1,0:T(8,128)S(1)}, f32[8,512,128,6]{2,1,3,0:T(8,128)S(1)}) fusion(f32[8,512]{1,0:T(8,128)S(1)} %multiply_bitcast_fusion.1, pred[8,6,512]{2,1,0:T(8,128)(4,1)S(1)} %copy.13, bf16[128,8,6,128]{0,3,2,1:T(8,128)(2,1)S(1)} %bitcast.52, bf16[512,8,128]{2,0,1:T(8,128)(2,1)} %all-gather.3.cloned.1.call-done), kind=kOutput, calls=%fused_computation.3 | convolution fusion | flops 814737408 | bytes 15269888 | tf_op jit(solution)/shard_map/while/body/eval_jaxpr/rkgd,jkd->kgrj/dot_general | solution.py:54
  47.1 0.0 copy-start
  47.1 4.5 %copy-done = f32[8,512,128,6]{2,1,3,0:T(8,128)} copy-done((f32[8,512,128,6]{2,1,3,0:T(8,128)}, f32[8,512,128,6]{2,1,3,0:T(8,128)S(1)}, u32[]{:S(2)}) %copy-start) | copy-done | bytes 12582936
  51.7 5.3 %fusion.1 = f32[8,6,128]{2,1,0:T(8,128)S(1)} fusion(f32[8,512,128,6]{2,1,3,0:T(8,128)S(1)} %get-tuple-element.26, f32[8,6,128]{2,1,0:T(8,128)S(1)} %get-tuple-element.24, f32[8,512]{1,0:T(8,128)S(1)} %multiply_bitcast_fusion.1, pred[8,6,512]{2,1,0:T(8,128)(4,1)S(1)} %copy.13), kind=kLoop, calls=%fused_computation.4 | loop fusion | flops 15722496 | bytes 12673024 | tf_op jit(solution)/shard_map/while/body/eval_jaxpr/reduce_sum | solution.py:67
  57.0 14.0 %all-gather.5.cloned.1.call-done = bf16[512,8,128]{0,2,1:T(8,128)(2,1)} async-done(((bf16[128,8,128]{0,2,1:T(8,128)(2,1)}), bf16[512,8,128]{0,2,1:T(8,128)(2,1)}) %all-gather.5.cloned.1.call-update) | async-done | bytes 1048592 | tf_op jit(solution)/shard_map/all_gather | solution.py:42
  71.0 10.4 %fusion.5 = bf16[128,8,6,128]{0,3,2,1:T(8,128)(2,1)S(1)} fusion(f32[8,512,128,6]{2,1,3,0:T(8,128)} %copy-done, f32[8,512]{1,0:T(8,128)S(1)} %convert_bitcast_fusion, f32[8,6,128]{2,1,0:T(8,128)S(1)} %get-tuple-element.24, f32[8,512]{1,0:T(8,128)S(1)} %multiply_bitcast_fusion.1, pred[8,6,512]{2,1,0:T(8,128)(4,1)S(1)} %copy.13, ...), kind=kOutput, calls=%fused_computation.9 | convolution fusion | flops 826540032 | bytes 15335424 | tf_op jit(solution)/shard_map/while/body/eval_jaxpr/kgrj,jkd->rkgd/dot_general | solution.py:72
  81.5 1.6 %copy.20 = bf16[128,6144]{1,0:T(8,128)(2,1)} copy(bf16[128,6144]{0,1:T(8,128)(2,1)S(1)} %bitcast.53) | data formatting | bytes 3145728 | tf_op jit(solution)/shard_map/reshape | solution.py:88
  (5 shorter events, 0.1 us)
Async XLA Ops:
  6.5 33.9 %all-gather.3.cloned.1.call-start = ((), (), s32[]{:S(2)}) async-start(), calls=%async_computation | async-start | bytes 1310720 | tf_op jit(solution)/shard_map/all_gather | solution.py:41
  8.5 62.5 %all-gather.5.cloned.1.call-start = ((), (), s32[]{:S(2)}) async-start(), calls=%async_computation.1 | async-start | bytes 1310720 | tf_op jit(solution)/shard_map/all_gather | solution.py:42
  47.1 4.6 %copy-start = (f32[8,512,128,6]{2,1,3,0:T(8,128)}, f32[8,512,128,6]{2,1,3,0:T(8,128)S(1)}, u32[]{:S(2)}) copy-start(f32[8,512,128,6]{2,1,3,0:T(8,128)S(1)} %get-tuple-element.26) | copy-start | bytes 37748740
Sparse Core Ops, SparseCore 0:
  8.9 30.8 all-gather.2
  41.4 29.6 all-gather.4
where the time goes:
time: 90.3 us; the launch traced here: 89.9 us
  blocking collectives  25.6 us (28%)
  matrix products  17.1 us (19%)
  waiting for transfers between devices  14.1 us (16%)
  local copies, waits for them, and re-layouts  13.5 us (15%)
  between operations  13.5 us (15%)
  other arithmetic  6.05 us (7%)
    all_gather x1, waiting for transfers between devices, local(): value_piece = lax.all_gather(value_heads, 'sp', axis=0, tiled=True)  14 us
    all_gather x1, blocking collectives, local(): key_piece_scale = lax.all_gather(key_tokens, 'sp', axis=0, tiled=True)  13.6 us
    all_gather x1, blocking collectives, local(): value_piece_scale = lax.all_gather(value_tokens, 'sp', axis=0, tiled=True)  12 us
    dot_general x1, matrix products, inner(): jnp.einsum('kgrj,jkd->rkgd', weighted, value_part, preferred_element_type...  10.4 us
    unnamed x5, local copies, waits for them, and re-layouts  9.33 us
    dot_general x1, matrix products, inner(): jnp.einsum('rkgd,jkd->kgrj', grouped, key_part, preferred_element_type=jn...  6.65 us
    reduce_sum x1, other arithmetic, inner(): jnp.sum(expo, axis=(4, 5)).reshape(KVH, per_group, tok_count)  5.32 us
  transfers between devices with their start and end apart: 2, of which 1 were waited for; matrix products, arithmetic and copies ran while one was open for 20% of the time, Pallas kernels for 0%

commit v1 on v0

v1 whole, which is shorter than its diff:
```python
import functools
import math

import jax
import jax.numpy as jnp
from jax import lax
from jax.experimental import pallas as pl
from jax.experimental.pallas import tpu as pltpu
from jax.sharding import PartitionSpec as P

NEGATIVE = -1e30
MESH = pl.DeviceIdType.MESH


def attention_kernel(
    devices, kv_heads, per_group, head, rows,
    q_hbm, k_hbm, v_hbm, key_scale_ref, value_scale_ref, masks_ref, out_hbm,
    q_ref, codes, scales, tops, totals, sums, stage,
    q_sem, own_sem, send_right, send_left, scale_right, scale_left,
    recv_sem, scale_recv, out_sem,
):
    me = lax.axis_index("sp")
    has_left = me > 0
    has_right = me < devices - 1
    last_step = jnp.maximum(me, devices - 1 - me)
    wide = per_group * head
    factor = math.log2(math.e) / math.sqrt(head)

    def own_copies(g):
        columns = pl.ds(pl.multiple_of(g * head, head), head)
        return (
            pltpu.make_async_copy(
                k_hbm.at[:, columns], codes.at[me, g, pl.ds(0, rows)], own_sem.at[g, 0]
            ),
            pltpu.make_async_copy(
                v_hbm.at[:, columns], codes.at[me, g, pl.ds(rows, rows)], own_sem.at[g, 1]
            ),
        )

    def q_copy():
        return pltpu.make_async_copy(q_hbm, q_ref, q_sem)

    def code_copy(tile, g, to, send):
        return pltpu.make_async_remote_copy(
            src_ref=codes.at[tile, g],
            dst_ref=codes.at[tile, g],
            send_sem=send.at[tile],
            recv_sem=recv_sem.at[tile, g],
            device_id={"sp": to},
            device_id_type=MESH,
        )

    def scale_copy(tile, to, send):
        return pltpu.make_async_remote_copy(
            src_ref=scales.at[tile],
            dst_ref=scales.at[tile],
            send_sem=send.at[tile],
            recv_sem=scale_recv.at[tile],
            device_id={"sp": to},
            device_id_type=MESH,
        )

    def out_copy(g):
        columns = pl.ds(pl.multiple_of(g * wide, wide), wide)
        return pltpu.make_async_copy(stage.at[:, columns], out_hbm.at[:, columns], out_sem.at[g])

    for g in range(kv_heads):
        for copy in own_copies(g):
            copy.start()
    q_copy().start()

    barrier = pltpu.get_barrier_semaphore()

    @pl.when(has_left)
    def _():
        pl.semaphore_signal(barrier, inc=1, device_id={"sp": me - 1}, device_id_type=MESH)

    @pl.when(has_right)
    def _():
        pl.semaphore_signal(barrier, inc=1, device_id={"sp": me + 1}, device_id_type=MESH)

    def column(ref):
        spread = jnp.broadcast_to(ref[...].astype(jnp.float32), (kv_heads, kv_heads))
        place = lax.broadcasted_iota(jnp.int32, (kv_heads, kv_heads), 0)
        other = lax.broadcasted_iota(jnp.int32, (kv_heads, kv_heads), 1)
        picked = jnp.sum(jnp.where(place == other, spread, 0.0), axis=1, keepdims=True)
        return jnp.broadcast_to(picked, (kv_heads, head))

    scales[me] = jnp.concatenate(
        [column(key_scale_ref), column(value_scale_ref)], axis=0
    ).astype(jnp.bfloat16)

    pl.semaphore_wait(barrier, has_left.astype(jnp.int32) + has_right.astype(jnp.int32))

    @pl.when(has_right)
    def _():
        scale_copy(me, me + 1, scale_right).start()

    @pl.when(has_left)
    def _():
        scale_copy(me, me - 1, scale_left).start()

    def send_own(g, carry):
        for copy in own_copies(g):
            copy.wait()

        @pl.when(has_right)
        def _():
            code_copy(me, g, me + 1, send_right).start()

        @pl.when(has_left)
        def _():
            code_copy(me, g, me - 1, send_left).start()

        return carry

    lax.fori_loop(0, kv_heads, send_own, 0)
    q_copy().wait()

    ones = jnp.ones((rows, head), jnp.bfloat16)

    def attend(tile, g, first):
        both = scales[tile].astype(jnp.float32)
        place = lax.broadcasted_iota(jnp.int32, both.shape, 0)
        key_scale = jnp.sum(jnp.where(place == g, both, 0.0), axis=0, keepdims=True)
        value_scale = jnp.sum(jnp.where(place == g + kv_heads, both, 0.0), axis=0, keepdims=True)
        key_scale = key_scale * factor
        queries = jnp.concatenate(
            [
                q_ref[:, pl.ds(pl.multiple_of((g * per_group + r) * head, head), head)]
                for r in range(per_group)
            ],
            axis=0,
        )
        keys = codes[tile, g, :rows, :]
        values = jnp.concatenate([codes[tile, g, rows:, :], ones], axis=1)
        raw = lax.dot_general(
            queries, keys, (((1,), (1,)), ((), ())), preferred_element_type=jnp.float32
        )
        expo, rescale = [], []
        for r in range(per_group):
            part = pl.ds(r * rows, rows)
            keep = masks_ref[g * per_group + r, me, tile]
            bias = jnp.where(keep > 0, 0.0, NEGATIVE).astype(jnp.float32)
            scores = raw[r * rows : (r + 1) * rows] * key_scale + bias
            top = jnp.broadcast_to(jnp.max(scores, axis=1, keepdims=True), (rows, head))
            if not first:
                before = tops[g, part, :]
                top = jnp.maximum(before, top)
                rescale.append(jnp.exp2(before - top))
            tops[g, part, :] = top
            expo.append(jnp.exp2(scores - top).astype(jnp.bfloat16))
        added = jnp.dot(
            jnp.concatenate(expo, axis=0), values, preferred_element_type=jnp.float32
        )
        for r in range(per_group):
            part = pl.ds(r * rows, rows)
            piece = added[r * rows : (r + 1) * rows]
            if first:
                sums[g, part, :] = piece[:, :head] * value_scale
                totals[g, part, :] = piece[:, head:]
            else:
                sums[g, part, :] = sums[g, part, :] * rescale[r] + piece[:, :head] * value_scale
                totals[g, part, :] = totals[g, part, :] * rescale[r] + piece[:, head:]

    def attend_own(g, carry):
        attend(me, g, True)
        return carry

    lax.fori_loop(0, kv_heads, attend_own, 0)

    def step_body(step, carry):
        left, right = me - step, me + step
        from_left, from_right = left >= 0, right <= devices - 1

        @pl.when(from_left)
        def _():
            scale_copy(left, me, scale_right).wait_recv()

            @pl.when(has_right)
            def _():
                scale_copy(left, me + 1, scale_right).start()

        @pl.when(from_right)
        def _():
            scale_copy(right, me, scale_left).wait_recv()

            @pl.when(has_left)
            def _():
                scale_copy(right, me - 1, scale_left).start()

        def chunk_body(g, inner):
            @pl.when(from_left)
            def _():
                code_copy(left, g, me, send_right).wait_recv()

                @pl.when(has_right)
                def _():
                    code_copy(left, g, me + 1, send_right).start()

            @pl.when(from_right)
            def _():
                code_copy(right, g, me, send_left).wait_recv()

                @pl.when(has_left)
                def _():
                    code_copy(right, g, me - 1, send_left).start()

            @pl.when(from_left)
            def _():
                attend(left, g, False)

            @pl.when(from_right)
            def _():
                attend(right, g, False)

            @pl.when(step == last_step)
            def _():
                for r in range(per_group):
                    part = pl.ds(r * rows, rows)
                    place = pl.ds(pl.multiple_of((g * per_group + r) * head, head), head)
                    stage[:, place] = (sums[g, part, :] / totals[g, part, :]).astype(jnp.bfloat16)
                out_copy(g).start()

            return inner

        lax.fori_loop(0, kv_heads, chunk_body, 0)
        return carry

    lax.fori_loop(1, last_step + 1, step_body, 0)

    def drain(tile, carry):
        @pl.when(jnp.logical_and(tile <= me, has_right))
        def _():
            scale_copy(tile, me + 1, scale_right).wait_send()
            pltpu.make_async_copy(codes.at[tile], codes.at[tile], send_right.at[tile]).wait()

        @pl.when(jnp.logical_and(tile >= me, has_left))
        def _():
            scale_copy(tile, me - 1, scale_left).wait_send()
            pltpu.make_async_copy(codes.at[tile], codes.at[tile], send_left.at[tile]).wait()

        return carry

    lax.fori_loop(0, devices, drain, 0)

    def flush(g, carry):
        out_copy(g).wait()
        return carry

    lax.fori_loop(0, kv_heads, flush, 0)


def local(devices, queries, key_codes, value_codes, key_scales, value_scales, masks):
    rows, width = queries.shape
    kv_heads = key_scales.shape[1]
    heads = masks.shape[0]
    head = width // heads
    per_group = heads // kv_heads
    tall = per_group * rows
    hbm = pl.BlockSpec(memory_space=pltpu.HBM)
    vmem = pl.BlockSpec(memory_space=pltpu.VMEM)
    smem = pl.BlockSpec(memory_space=pltpu.SMEM)
    dma = pltpu.SemaphoreType.DMA
    scores = heads * rows * rows * devices
    return pl.pallas_call(
        functools.partial(attention_kernel, devices, kv_heads, per_group, head, rows),
        out_shape=jax.ShapeDtypeStruct((rows, width), jnp.bfloat16),
        in_specs=[hbm, hbm, hbm, vmem, vmem, smem],
        out_specs=hbm,
        scratch_shapes=[
            pltpu.VMEM((rows, width), jnp.bfloat16),
            pltpu.VMEM((devices, kv_heads, 2 * rows, head), jnp.bfloat16),
            pltpu.VMEM((devices, 2 * kv_heads, head), jnp.bfloat16),
            pltpu.VMEM((kv_heads, tall, head), jnp.float32),
            pltpu.VMEM((kv_heads, tall, head), jnp.float32),
            pltpu.VMEM((kv_heads, tall, head), jnp.float32),
            pltpu.VMEM((rows, width), jnp.bfloat16),
            dma,
            dma((kv_heads, 2)),
            dma((devices,)),
            dma((devices,)),
            dma((devices,)),
            dma((devices,)),
            dma((devices, kv_heads)),
            dma((devices,)),
            dma((kv_heads,)),
        ],
        compiler_params=pltpu.CompilerParams(
            collective_id=0, has_side_effects=True, vmem_limit_bytes=48 * 1024 * 1024
        ),
        cost_estimate=pl.CostEstimate(
            flops=4 * scores * head, bytes_accessed=4 * rows * width, transcendentals=scores
        ),
    )(queries, key_codes, value_codes, key_scales, value_scales, masks)


def solution(mesh):
    both = P(("clip", "sp"), None)
    return jax.shard_map(
        functools.partial(local, mesh.shape["sp"]),
        mesh=mesh,
        in_specs=(both, both, both, both, both, P("clip", None, None)),
        out_specs=both,
        check_vma=False,
    )
```

time: 90.3 us -> 49.7 us (0.55)
  Pallas kernels: 0 us -> 42.8 us
  blocking collectives: 25.6 us -> 0 us
  matrix products: 17.1 us -> 0 us
  waiting for transfers between devices: 14.1 us -> 0 us
  between operations: 13.5 us -> 0.03 us
  local copies, waits for them, and re-layouts: 13.5 us -> 6.56 us
  other arithmetic: 6.05 us -> 0 us
    pallas_call x0 -> x1, Pallas kernels: none -> 42.8 us  [local(): pl.pallas_call(functools.partial(attention_kernel, devices, kv_heads, per...]
    all_gather x2 -> x0, blocking collectives: 25.6 us -> none  [the longest x1 13.6 us: local(): key_piece_scale = lax.all_gather(key_tokens, 'sp', axis=0, tiled=True)]
    dot_general x2 -> x0, matrix products: 17.1 us -> none  [the longest x1 10.4 us: inner(): jnp.einsum('kgrj,jkd->rkgd', weighted, value_part, preferred_element_type...]
    all_gather x2 -> x0, waiting for transfers between devices: 14 us -> none  [the longest x1 14 us: local(): value_piece = lax.all_gather(value_heads, 'sp', axis=0, tiled=True)]
    reduce_sum x1 -> x0, other arithmetic: 5.32 us -> none  [inner(): jnp.sum(expo, axis=(4, 5)).reshape(KVH, per_group, tok_count)]
    reshape x4 -> x0, local copies, waits for them, and re-layouts: 3.88 us -> none  [the longest x1 1.57 us: local(): return normed.astype(jnp.bfloat16).reshape(tok_count, QH * HD)]
    unnamed x5 -> x12, local copies, waits for them, and re-layouts: 9.33 us -> 6.56 us
  transfers between devices with their start and end apart: 2 -> 0, of which waited for: 1 -> 0; matrix products, arithmetic and copies ran while one was open for 20% -> 0% of each run, Pallas kernels for 0% -> 0%
where the time goes in v1:
time: 49.7 us; the launch traced here: 49.4 us
  Pallas kernels  42.8 us (86%)
  local copies, waits for them, and re-layouts  6.56 us (13%)
    pallas_call x1, Pallas kernels, local(): pl.pallas_call(functools.partial(attention_kernel, devices, kv_heads, per...  42.8 us
    unnamed x12, local copies, waits for them, and re-layouts  6.56 us

profile of v1, /device:TPU:0, one launch (start us, length us, event | category | flops | bytes accessed | tf_op | source)
XLA Modules:
  0.0 49.4 jit_solution(3763769846189553693)
XLA Ops:
  0.0 0.8 %copy.7.masks_ref = s32[48,4,4]{2,1,0:T(4,128)S(1)} copy(s32[48,4,4]{0,2,1:T(4,128)} %param.11) | data formatting | bytes 6144 | tf_op args[5]
  0.8 0.0 copy-start
  0.8 1.4 %copy-done = bf16[128,6144]{1,0:T(8,128)(2,1)S(1)} copy-done((bf16[128,6144]{1,0:T(8,128)(2,1)S(1)}, bf16[128,6144]{1,0:T(8,128)(2,1)}, u32[]{:S(2)}) %copy-start) | copy-done | bytes 1572888
  2.2 0.0 copy-start.1
  2.2 0.9 %copy-done.1 = bf16[128,1024]{1,0:T(8,128)(2,1)S(1)} copy-done((bf16[128,1024]{1,0:T(8,128)(2,1)S(1)}, bf16[128,1024]{1,0:T(8,128)(2,1)}, u32[]{:S(2)}) %copy-start.1) | copy-done | bytes 262168
  3.2 0.0 copy-start.2
  3.2 0.9 %copy-done.2 = bf16[128,1024]{1,0:T(8,128)(2,1)S(1)} copy-done((bf16[128,1024]{1,0:T(8,128)(2,1)S(1)}, bf16[128,1024]{1,0:T(8,128)(2,1)}, u32[]{:S(2)}) %copy-start.2) | copy-done | bytes 262168
  4.1 0.0 copy-start.3
  4.1 0.7 %copy-done.3 = bf16[1,8]{1,0:T(2,128)(2,1)S(1)} copy-done((bf16[1,8]{1,0:T(2,128)(2,1)S(1)}, bf16[1,8]{1,0:T(2,128)(2,1)}, u32[]{:S(2)}) %copy-start.3) | copy-done | bytes 40
  4.8 0.0 copy-start.4
  4.8 0.7 %copy-done.4 = bf16[1,8]{1,0:T(2,128)(2,1)S(1)} copy-done((bf16[1,8]{1,0:T(2,128)(2,1)S(1)}, bf16[1,8]{1,0:T(2,128)(2,1)}, u32[]{:S(2)}) %copy-start.4) | copy-done | bytes 40
  5.4 42.8 %shard_map.64 = bf16[128,6144]{1,0:T(8,128)(2,1)S(1)} custom-call(bf16[128,6144]{1,0:T(8,128)(2,1)S(1)} %copy-done, bf16[128,1024]{1,0:T(8,128)(2,1)S(1)} %copy-done.1, bf16[128,1024]{1,0:T(8,128)(2,1)S(1)} %copy-done.2, bf16[1,8]{1,0:T(2,128)(2,1)S(1)} %copy-done.3, bf16[1,8]{1,0:T(2,128)(2,1)S(1)} %copy-done.4, s32[48,4,4]{2,1,0:T(4,128)S(1)} %copy.7.masks_ref), custom_call_target="tpu_custom_call" | custom-call | flops 1610612736 | bytes 3145728 | tf_op jit(solution)/shard_map/pallas_call | solution.py:266
  48.3 1.1 %copy.9 = bf16[128,6144]{1,0:T(8,128)(2,1)} copy(bf16[128,6144]{1,0:T(8,128)(2,1)S(1)} %shard_map.64) | data formatting | bytes 3145728
Async XLA Ops:
  0.8 1.4 %copy-start = (bf16[128,6144]{1,0:T(8,128)(2,1)S(1)}, bf16[128,6144]{1,0:T(8,128)(2,1)}, u32[]{:S(2)}) copy-start(bf16[128,6144]{1,0:T(8,128)(2,1)} %q_hbm.1) | copy-start | bytes 4718596
  2.2 0.9 %copy-start.1 = (bf16[128,1024]{1,0:T(8,128)(2,1)S(1)}, bf16[128,1024]{1,0:T(8,128)(2,1)}, u32[]{:S(2)}) copy-start(bf16[128,1024]{1,0:T(8,128)(2,1)} %k_hbm.1) | copy-start | bytes 786436
  3.2 0.9 %copy-start.2 = (bf16[128,1024]{1,0:T(8,128)(2,1)S(1)}, bf16[128,1024]{1,0:T(8,128)(2,1)}, u32[]{:S(2)}) copy-start(bf16[128,1024]{1,0:T(8,128)(2,1)} %v_hbm.1) | copy-start | bytes 786436
  4.1 0.7 %copy-start.3 = (bf16[1,8]{1,0:T(2,128)(2,1)S(1)}, bf16[1,8]{1,0:T(2,128)(2,1)}, u32[]{:S(2)}) copy-start(bf16[1,8]{1,0:T(2,128)(2,1)} %key_scale_ref.1) | copy-start | bytes 52
  4.8 0.7 %copy-start.4 = (bf16[1,8]{1,0:T(2,128)(2,1)S(1)}, bf16[1,8]{1,0:T(2,128)(2,1)}, u32[]{:S(2)}) copy-start(bf16[1,8]{1,0:T(2,128)(2,1)} %value_scale_ref.1) | copy-start | bytes 52

commit v2 on v1

v2 whole, which is shorter than its diff:
```python
import functools
import math

import jax
import jax.numpy as jnp
from jax import lax
from jax.experimental import pallas as pl
from jax.experimental.pallas import tpu as pltpu
from jax.sharding import PartitionSpec as P

NEGATIVE = -1e30
MESH = pl.DeviceIdType.MESH


def attention_kernel(
    devices, kv_heads, per_group, head, rows,
    q_hbm, k_hbm, v_hbm, key_scale_hbm, value_scale_hbm, masks_hbm, out_hbm,
    q_ref, codes, scales, tops, totals, sums, stage, key_scale_ref, value_scale_ref, masks_ref,
    q_sem, small_sem, own_sem, send_right, send_left, scale_right, scale_left,
    recv_sem, scale_recv, out_sem,
):
    me = lax.axis_index("sp")
    to_right = lax.rem(me + 1, devices)
    to_left = lax.rem(me + devices - 1, devices)
    full = (devices - 1) // 2
    split = devices % 2 == 0
    half = kv_heads // 2
    wide = per_group * head
    factor = math.log2(math.e) / math.sqrt(head)

    barrier = pltpu.get_barrier_semaphore()
    for neighbour in (to_left, to_right):
        pl.semaphore_signal(barrier, inc=1, device_id={"sp": neighbour}, device_id_type=MESH)

    def own_copies(g):
        columns = pl.ds(pl.multiple_of(g * head, head), head)
        return (
            pltpu.make_async_copy(
                k_hbm.at[:, columns], codes.at[me, g, pl.ds(0, rows)], own_sem.at[g, 0]
            ),
            pltpu.make_async_copy(
                v_hbm.at[:, columns], codes.at[me, g, pl.ds(rows, rows)], own_sem.at[g, 1]
            ),
        )

    def q_copy():
        return pltpu.make_async_copy(q_hbm, q_ref, q_sem)

    def small_copies():
        return (
            pltpu.make_async_copy(key_scale_hbm, key_scale_ref, small_sem.at[0]),
            pltpu.make_async_copy(value_scale_hbm, value_scale_ref, small_sem.at[1]),
            pltpu.make_async_copy(masks_hbm, masks_ref, small_sem.at[2]),
        )

    def code_copy(tile, g, to, send):
        return pltpu.make_async_remote_copy(
            src_ref=codes.at[tile, g],
            dst_ref=codes.at[tile, g],
            send_sem=send.at[tile],
            recv_sem=recv_sem.at[tile, g],
            device_id={"sp": to},
            device_id_type=MESH,
        )

    def scale_copy(tile, to, send):
        return pltpu.make_async_remote_copy(
            src_ref=scales.at[tile],
            dst_ref=scales.at[tile],
            send_sem=send.at[tile],
            recv_sem=scale_recv.at[tile],
            device_id={"sp": to},
            device_id_type=MESH,
        )

    def out_copy(g):
        columns = pl.ds(pl.multiple_of(g * wide, wide), wide)
        return pltpu.make_async_copy(stage.at[:, columns], out_hbm.at[:, columns], out_sem.at[g])

    for copy in small_copies():
        copy.start()
    for g in range(kv_heads):
        for copy in own_copies(g):
            copy.start()
    q_copy().start()

    def column(ref):
        spread = jnp.broadcast_to(ref[...].astype(jnp.float32), (kv_heads, kv_heads))
        place = lax.broadcasted_iota(jnp.int32, (kv_heads, kv_heads), 0)
        other = lax.broadcasted_iota(jnp.int32, (kv_heads, kv_heads), 1)
        picked = jnp.sum(jnp.where(place == other, spread, 0.0), axis=1, keepdims=True)
        return jnp.broadcast_to(picked, (kv_heads, head))

    for copy in small_copies():
        copy.wait()
    scales[me] = jnp.concatenate(
        [column(key_scale_ref), column(value_scale_ref)], axis=0
    ).astype(jnp.bfloat16)

    pl.semaphore_wait(barrier, 2)

    def send_scales(tile, hop, rightward):
        if rightward:
            @pl.when(hop < (full + 1 if split else full))
            def _():
                scale_copy(tile, to_right, scale_right).start()
        else:
            @pl.when(hop < full)
            def _():
                scale_copy(tile, to_left, scale_left).start()

    def send_codes(tile, g, hop, rightward):
        go = hop < full
        if split:
            mine = g < half if rightward else g >= half
            go = jnp.logical_or(go, jnp.logical_and(hop == full, mine))

        @pl.when(go)
        def _():
            if rightward:
                code_copy(tile, g, to_right, send_right).start()
            else:
                code_copy(tile, g, to_left, send_left).start()

    send_scales(me, 0, True)
    send_scales(me, 0, False)

    def send_own(g, carry):
        for copy in own_copies(g):
            copy.wait()
        send_codes(me, g, 0, True)
        send_codes(me, g, 0, False)
        return carry

    lax.fori_loop(0, kv_heads, send_own, 0)
    q_copy().wait()

    ones = jnp.ones((rows, head), jnp.bfloat16)

    def attend(tile, g, first=False, last=False):
        both = scales[tile].astype(jnp.float32)
        place = lax.broadcasted_iota(jnp.int32, both.shape, 0)
        key_scale = jnp.sum(jnp.where(place == g, both, 0.0), axis=0, keepdims=True)
        value_scale = jnp.sum(jnp.where(place == g + kv_heads, both, 0.0), axis=0, keepdims=True)
        key_scale = key_scale * factor
        queries = jnp.concatenate(
            [
                q_ref[:, pl.ds(pl.multiple_of((g * per_group + r) * head, head), head)]
                for r in range(per_group)
            ],
            axis=0,
        )
        keys = codes[tile, g, :rows, :]
        values = jnp.concatenate([codes[tile, g, rows:, :], ones], axis=1)
        raw = lax.dot_general(
            queries, keys, (((1,), (1,)), ((), ())), preferred_element_type=jnp.float32
        )
        expo, rescale = [], []
        for r in range(per_group):
            part = pl.ds(r * rows, rows)
            keep = masks_ref[me, tile, g * per_group + r]
            bias = jnp.where(keep > 0, 0.0, NEGATIVE).astype(jnp.float32)
            scores = raw[r * rows : (r + 1) * rows] * key_scale + bias
            top = jnp.broadcast_to(jnp.max(scores, axis=1, keepdims=True), (rows, head))
            if not first:
                before = tops[g, part, :]
                top = jnp.maximum(before, top)
                rescale.append(jnp.exp2(before - top))
            if not last:
                tops[g, part, :] = top
            expo.append(jnp.exp2(scores - top).astype(jnp.bfloat16))
        added = jnp.dot(
            jnp.concatenate(expo, axis=0), values, preferred_element_type=jnp.float32
        )
        for r in range(per_group):
            part = pl.ds(r * rows, rows)
            piece = added[r * rows : (r + 1) * rows]
            product = piece[:, :head] * value_scale
            total = piece[:, head:]
            if not first:
                product = product + sums[g, part, :] * rescale[r]
                total = total + totals[g, part, :] * rescale[r]
            if last:
                place = pl.ds(pl.multiple_of((g * per_group + r) * head, head), head)
                stage[:, place] = (product / total).astype(jnp.bfloat16)
            else:
                sums[g, part, :] = product
                totals[g, part, :] = total
        if last:
            out_copy(g).start()

    def attend_own(g, carry):
        attend(me, g, first=True)
        return carry

    lax.fori_loop(0, kv_heads, attend_own, 0)

    def step_body(step, carry):
        left = lax.rem(me - step + devices, devices)
        right = lax.rem(me + step, devices)
        scale_copy(left, to_right, scale_right).wait_recv()
        send_scales(left, step, True)
        scale_copy(right, to_left, scale_left).wait_recv()
        send_scales(right, step, False)

        def chunk_body(g, inner):
            code_copy(left, g, to_right, send_right).wait_recv()
            send_codes(left, g, step, True)
            code_copy(right, g, to_left, send_left).wait_recv()
            send_codes(right, g, step, False)
            attend(left, g)
            attend(right, g)
            return inner

        lax.fori_loop(0, kv_heads, chunk_body, 0)
        return carry

    lax.fori_loop(1, full + 1, step_body, 0)

    if split:
        across = lax.rem(me + devices // 2, devices)
        scale_copy(across, to_right, scale_right).wait_recv()

        def across_body(g, carry):
            code_copy(across, g, to_right, send_right).wait_recv()
            attend(across, g, last=True)
            code_copy(across, g + half, to_left, send_left).wait_recv()
            attend(across, g + half, last=True)
            return carry

        lax.fori_loop(0, half, across_body, 0)
    else:

        def finish(g, carry):
            for r in range(per_group):
                part = pl.ds(r * rows, rows)
                place = pl.ds(pl.multiple_of((g * per_group + r) * head, head), head)
                stage[:, place] = (sums[g, part, :] / totals[g, part, :]).astype(jnp.bfloat16)
            out_copy(g).start()
            return carry

        lax.fori_loop(0, kv_heads, finish, 0)

    def drain(hop, carry):
        left = lax.rem(me - hop + devices, devices)
        right = lax.rem(me + hop, devices)
        scale_copy(left, to_right, scale_right).wait_send()
        scale_copy(right, to_left, scale_left).wait_send()
        pltpu.make_async_copy(codes.at[left], codes.at[left], send_right.at[left]).wait()
        pltpu.make_async_copy(codes.at[right], codes.at[right], send_left.at[right]).wait()
        return carry

    lax.fori_loop(0, full, drain, 0)
    if split:
        left = lax.rem(me - full + devices, devices)
        right = lax.rem(me + full, devices)
        first, second = pl.ds(0, half), pl.ds(half, half)
        scale_copy(left, to_right, scale_right).wait_send()
        pltpu.make_async_copy(
            codes.at[left, first], codes.at[left, first], send_right.at[left]
        ).wait()
        pltpu.make_async_copy(
            codes.at[right, second], codes.at[right, second], send_left.at[right]
        ).wait()

    def flush(g, carry):
        out_copy(g).wait()
        return carry

    lax.fori_loop(0, kv_heads, flush, 0)


def local(devices, queries, key_codes, value_codes, key_scales, value_scales, masks):
    rows, width = queries.shape
    kv_heads = key_scales.shape[1]
    masks = jnp.transpose(masks, (1, 2, 0))
    heads = masks.shape[2]
    head = width // heads
    per_group = heads // kv_heads
    tall = per_group * rows
    hbm = pl.BlockSpec(memory_space=pltpu.HBM)
    dma = pltpu.SemaphoreType.DMA
    scores = heads * rows * rows * devices
    return pl.pallas_call(
        functools.partial(attention_kernel, devices, kv_heads, per_group, head, rows),
        out_shape=jax.ShapeDtypeStruct((rows, width), jnp.bfloat16),
        in_specs=[hbm] * 6,
        out_specs=hbm,
        scratch_shapes=[
            pltpu.VMEM((rows, width), jnp.bfloat16),
            pltpu.VMEM((devices, kv_heads, 2 * rows, head), jnp.bfloat16),
            pltpu.VMEM((devices, 2 * kv_heads, head), jnp.bfloat16),
            pltpu.VMEM((kv_heads, tall, head), jnp.float32),
            pltpu.VMEM((kv_heads, tall, head), jnp.float32),
            pltpu.VMEM((kv_heads, tall, head), jnp.float32),
            pltpu.VMEM((rows, width), jnp.bfloat16),
            pltpu.VMEM(key_scales.shape, jnp.bfloat16),
            pltpu.VMEM(value_scales.shape, jnp.bfloat16),
            pltpu.SMEM(masks.shape, jnp.int32),
            dma,
            dma((3,)),
            dma((kv_heads, 2)),
            dma((devices,)),
            dma((devices,)),
            dma((devices,)),
            dma((devices,)),
            dma((devices, kv_heads)),
            dma((devices,)),
            dma((kv_heads,)),
        ],
        compiler_params=pltpu.CompilerParams(
            collective_id=0, has_side_effects=True, vmem_limit_bytes=63 * 1024 * 1024
        ),
        cost_estimate=pl.CostEstimate(
            flops=4 * scores * head, bytes_accessed=4 * rows * width, transcendentals=scores
        ),
    )(queries, key_codes, value_codes, key_scales, value_scales, masks)


def solution(mesh):
    both = P(("clip", "sp"), None)
    return jax.shard_map(
        functools.partial(local, mesh.shape["sp"]),
        mesh=mesh,
        in_specs=(both, both, both, both, both, P("clip", None, None)),
        out_specs=both,
        check_vma=False,
    )
```

time: 49.7 us -> 44.4 us (0.89)
  local copies, waits for them, and re-layouts: 6.56 us -> 2.69 us
  Pallas kernels: 42.8 us -> 41.5 us
    unnamed x12 -> x1, local copies, waits for them, and re-layouts: 6.56 us -> 2.69 us
    pallas_call x1, Pallas kernels: 42.8 us -> 41.5 us  [local(): pl.pallas_call(functools.partial(attention_kernel, devices, kv_heads, per...]
where the time goes in v2:
time: 44.4 us; the launch traced here: 44.2 us
  Pallas kernels  41.5 us (93%)
  local copies, waits for them, and re-layouts  2.69 us (6%)
    pallas_call x1, Pallas kernels, local(): pl.pallas_call(functools.partial(attention_kernel, devices, kv_heads, per...  41.5 us
    unnamed x1, local copies, waits for them, and re-layouts  2.69 us

profile of v2, /device:TPU:0, one launch (start us, length us, event | category | flops | bytes accessed | tf_op | source)
XLA Modules:
  0.0 44.2 jit_solution(11803757469989128895)
XLA Ops:
  0.0 41.5 %shard_map.64 = bf16[128,6144]{1,0:T(8,128)(2,1)} custom-call(bf16[128,6144]{1,0:T(8,128)(2,1)} %q_hbm.1, bf16[128,1024]{1,0:T(8,128)(2,1)} %k_hbm.1, bf16[128,1024]{1,0:T(8,128)(2,1)} %v_hbm.1, bf16[1,8]{1,0:T(2,128)(2,1)} %key_scale_hbm.1, bf16[1,8]{1,0:T(2,128)(2,1)} %value_scale_hbm.1, s32[4,4,48]{2,1,0:T(4,128)} %bitcast.1), custom_call_target="tpu_custom_call" | custom-call | flops 1610612736 | bytes 3145728 | tf_op jit(solution)/shard_map/pallas_call | solution.py:284
  41.5 2.7 %copy.8 = bf16[128,6144]{1,0:T(8,128)(2,1)} copy(bf16[128,6144]{1,0:T(8,128)(2,1)} %shard_map.64) | data formatting | bytes 3145728

commit v3 on v1

v3 whole, which is shorter than its diff:
```python
import functools
import math

import jax
import jax.numpy as jnp
from jax import lax
from jax.experimental import pallas as pl
from jax.experimental.pallas import tpu as pltpu
from jax.sharding import PartitionSpec as P

NEGATIVE = -1e30
MESH = pl.DeviceIdType.MESH


def attention_kernel(
    devices, kv_heads, per_group, head, rows,
    q_hbm, k_hbm, v_hbm, key_scale_hbm, value_scale_hbm, masks_hbm, out_hbm,
    q_ref, q_turned, codes, scales, tops, totals, sums, stage,
    key_scale_ref, value_scale_ref, masks_ref,
    q_sem, small_sem, own_sem, send_right, send_left, scale_right, scale_left,
    recv_sem, scale_recv, out_sem,
):
    me = lax.axis_index("sp")
    has_left = me > 0
    has_right = me < devices - 1
    middle = jnp.logical_and(has_left, has_right)
    last_step = jnp.maximum(me, devices - 1 - me)
    wide = per_group * head
    pair = 2 if per_group % 2 == 0 else 1
    factor = math.log2(math.e) / math.sqrt(head)

    barrier = pltpu.get_barrier_semaphore()

    @pl.when(has_left)
    def _():
        pl.semaphore_signal(barrier, inc=1, device_id={"sp": me - 1}, device_id_type=MESH)

    @pl.when(has_right)
    def _():
        pl.semaphore_signal(barrier, inc=1, device_id={"sp": me + 1}, device_id_type=MESH)

    def own_copies(g):
        columns = pl.ds(pl.multiple_of(g * head, head), head)
        return (
            pltpu.make_async_copy(
                k_hbm.at[:, columns], codes.at[me, g, pl.ds(0, rows)], own_sem.at[g, 0]
            ),
            pltpu.make_async_copy(
                v_hbm.at[:, columns], codes.at[me, g, pl.ds(rows, rows)], own_sem.at[g, 1]
            ),
        )

    def q_copy():
        return pltpu.make_async_copy(q_hbm, q_ref, q_sem)

    def small_copies():
        return (
            pltpu.make_async_copy(key_scale_hbm, key_scale_ref, small_sem.at[0]),
            pltpu.make_async_copy(value_scale_hbm, value_scale_ref, small_sem.at[1]),
            pltpu.make_async_copy(masks_hbm, masks_ref, small_sem.at[2]),
        )

    def code_copy(tile, g, to, send):
        return pltpu.make_async_remote_copy(
            src_ref=codes.at[tile, g],
            dst_ref=codes.at[tile, g],
            send_sem=send.at[tile],
            recv_sem=recv_sem.at[tile, g],
            device_id={"sp": to},
            device_id_type=MESH,
        )

    def scale_copy(tile, to, send):
        return pltpu.make_async_remote_copy(
            src_ref=scales.at[tile],
            dst_ref=scales.at[tile],
            send_sem=send.at[tile],
            recv_sem=scale_recv.at[tile],
            device_id={"sp": to},
            device_id_type=MESH,
        )

    def out_copy(g):
        columns = pl.ds(pl.multiple_of(g * wide, wide), wide)
        return pltpu.make_async_copy(stage.at[:, columns], out_hbm.at[:, columns], out_sem.at[g])

    for copy in small_copies():
        copy.start()
    for g in range(kv_heads):
        for copy in own_copies(g):
            copy.start()
    q_copy().start()

    def column(ref):
        spread = jnp.broadcast_to(ref[...].astype(jnp.float32), (kv_heads, kv_heads))
        place = lax.broadcasted_iota(jnp.int32, (kv_heads, kv_heads), 0)
        other = lax.broadcasted_iota(jnp.int32, (kv_heads, kv_heads), 1)
        picked = jnp.sum(jnp.where(place == other, spread, 0.0), axis=1, keepdims=True)
        return jnp.broadcast_to(picked, (kv_heads, head))

    for copy in small_copies():
        copy.wait()
    scales[me] = jnp.concatenate(
        [column(key_scale_ref), column(value_scale_ref)], axis=0
    ).astype(jnp.bfloat16)

    pl.semaphore_wait(barrier, has_left.astype(jnp.int32) + has_right.astype(jnp.int32))

    @pl.when(has_right)
    def _():
        scale_copy(me, me + 1, scale_right).start()

    @pl.when(has_left)
    def _():
        scale_copy(me, me - 1, scale_left).start()

    def send_own(g, carry):
        for copy in own_copies(g):
            copy.wait()

        @pl.when(has_right)
        def _():
            code_copy(me, g, me + 1, send_right).start()

        @pl.when(has_left)
        def _():
            code_copy(me, g, me - 1, send_left).start()

        return carry

    lax.fori_loop(0, kv_heads, send_own, 0)
    q_copy().wait()

    ones = jnp.ones((16, rows), jnp.bfloat16)

    def attend(tile, g, first=False):
        both = scales[tile].astype(jnp.float32)
        place = lax.broadcasted_iota(jnp.int32, both.shape, 0)
        key_scale = jnp.sum(jnp.where(place == g, both, 0.0), axis=0, keepdims=True)
        value_scale = jnp.sum(jnp.where(place == g + kv_heads, both, 0.0), axis=0, keepdims=True)
        key_scale = jnp.concatenate([key_scale * factor] * pair, axis=1)
        value_scale = jnp.concatenate([value_scale] * pair, axis=1)
        keys = codes[tile, g, :rows, :]
        values = jnp.concatenate([jnp.transpose(codes[tile, g, rows:, :]), ones], axis=0)
        for r in range(0, per_group, pair):
            columns = pl.ds(r * rows, pair * rows)
            if first:
                queries = jnp.concatenate(
                    [
                        jnp.transpose(
                            q_ref[:, pl.ds(pl.multiple_of((g * per_group + o) * head, head), head)]
                        )
                        for o in range(r, r + pair)
                    ],
                    axis=1,
                )
                q_turned[g, :, columns] = queries
            else:
                queries = q_turned[g, :, columns]
            raw = jnp.dot(keys, queries, preferred_element_type=jnp.float32)
            bias = jnp.concatenate(
                [
                    jnp.full(
                        (1, rows),
                        jnp.where(masks_ref[me, tile, g * per_group + o] > 0, 0.0, NEGATIVE),
                        jnp.float32,
                    )
                    for o in range(r, r + pair)
                ],
                axis=1,
            )
            top = jnp.max(raw, axis=0, keepdims=True) * key_scale + bias
            if not first:
                before = tops[g, :, columns]
                top = jnp.maximum(before, top)
                rescale = jnp.exp2(before - top)
            tops[g, :, columns] = top
            expo = jnp.exp2(raw * key_scale - (top - bias)).astype(jnp.bfloat16)
            added = jnp.dot(values, expo, preferred_element_type=jnp.float32)
            product = added[:head] * value_scale
            total = added[head : head + 1]
            if not first:
                product = product + sums[g, :, columns] * rescale
                total = total + totals[g, :, columns] * rescale
            sums[g, :, columns] = product
            totals[g, :, columns] = total

    def finish(g):
        for r in range(per_group):
            columns = pl.ds(r * rows, rows)
            place = pl.ds(pl.multiple_of((g * per_group + r) * head, head), head)
            normed = sums[g, :, columns] * (1.0 / totals[g, :, columns])
            stage[:, place] = jnp.transpose(normed).astype(jnp.bfloat16)
        out_copy(g).start()

    lag = middle.astype(jnp.int32)

    def step_body(step, carry):
        left, right = me - step, me + step
        arrives = jnp.logical_and(step > 0, step <= last_step)
        from_left = jnp.logical_and(arrives, left >= 0)
        from_right = jnp.logical_and(arrives, right <= devices - 1)
        span = step - lag
        near, far = me - span, me + span

        @pl.when(from_left)
        def _():
            scale_copy(left, me, scale_right).wait_recv()

            @pl.when(has_right)
            def _():
                scale_copy(left, me + 1, scale_right).start()

        @pl.when(from_right)
        def _():
            scale_copy(right, me, scale_left).wait_recv()

            @pl.when(has_left)
            def _():
                scale_copy(right, me - 1, scale_left).start()

        def chunk_body(g, inner):
            @pl.when(from_left)
            def _():
                code_copy(left, g, me, send_right).wait_recv()

                @pl.when(has_right)
                def _():
                    code_copy(left, g, me + 1, send_right).start()

            @pl.when(from_right)
            def _():
                code_copy(right, g, me, send_left).wait_recv()

                @pl.when(has_left)
                def _():
                    code_copy(right, g, me - 1, send_left).start()

            @pl.when(span == 0)
            def _():
                attend(me, g, first=True)

            @pl.when(jnp.logical_and(span > 0, near >= 0))
            def _():
                attend(near, g)

            @pl.when(jnp.logical_and(span > 0, far <= devices - 1))
            def _():
                attend(far, g)

            @pl.when(span == last_step)
            def _():
                finish(g)

            return inner

        lax.fori_loop(0, kv_heads, chunk_body, 0)
        return carry

    lax.fori_loop(lag, last_step + lag + 1, step_body, 0)

    def drain(tile, carry):
        @pl.when(jnp.logical_and(tile <= me, has_right))
        def _():
            scale_copy(tile, me + 1, scale_right).wait_send()
            pltpu.make_async_copy(codes.at[tile], codes.at[tile], send_right.at[tile]).wait()

        @pl.when(jnp.logical_and(tile >= me, has_left))
        def _():
            scale_copy(tile, me - 1, scale_left).wait_send()
            pltpu.make_async_copy(codes.at[tile], codes.at[tile], send_left.at[tile]).wait()

        return carry

    lax.fori_loop(0, devices, drain, 0)

    def flush(g, carry):
        out_copy(g).wait()
        return carry

    lax.fori_loop(0, kv_heads, flush, 0)


def place_kernel(pieces, from_ref, to_ref, sems):
    rows = from_ref.shape[0] // pieces
    copies = [
        pltpu.make_async_copy(
            from_ref.at[pl.ds(p * rows, rows)], to_ref.at[pl.ds(p * rows, rows)], sems.at[p]
        )
        for p in range(pieces)
    ]
    for copy in copies:
        copy.start()
    for copy in copies:
        copy.wait()


def local(devices, queries, key_codes, value_codes, key_scales, value_scales, masks):
    rows, width = queries.shape
    kv_heads = key_scales.shape[1]
    masks = jnp.transpose(masks, (1, 2, 0))
    heads = masks.shape[2]
    head = width // heads
    per_group = heads // kv_heads
    tall = per_group * rows
    pieces = rows // 16
    hbm = pl.BlockSpec(memory_space=pltpu.HBM)
    dma = pltpu.SemaphoreType.DMA
    scores = heads * rows * rows * devices
    attended = pl.pallas_call(
        functools.partial(attention_kernel, devices, kv_heads, per_group, head, rows),
        out_shape=jax.ShapeDtypeStruct((rows, width), jnp.bfloat16),
        in_specs=[hbm] * 6,
        out_specs=hbm,
        scratch_shapes=[
            pltpu.VMEM((rows, width), jnp.bfloat16),
            pltpu.VMEM((kv_heads, head, tall), jnp.bfloat16),
            pltpu.VMEM((devices, kv_heads, 2 * rows, head), jnp.bfloat16),
            pltpu.VMEM((devices, 2 * kv_heads, head), jnp.bfloat16),
            pltpu.VMEM((kv_heads, 1, tall), jnp.float32),
            pltpu.VMEM((kv_heads, 1, tall), jnp.float32),
            pltpu.VMEM((kv_heads, head, tall), jnp.float32),
            pltpu.VMEM((rows, width), jnp.bfloat16),
            pltpu.VMEM(key_scales.shape, jnp.bfloat16),
            pltpu.VMEM(value_scales.shape, jnp.bfloat16),
            pltpu.SMEM(masks.shape, jnp.int32),
            dma,
            dma((3,)),
            dma((kv_heads, 2)),
            dma((devices,)),
            dma((devices,)),
            dma((devices,)),
            dma((devices,)),
            dma((devices, kv_heads)),
            dma((devices,)),
            dma((kv_heads,)),
        ],
        compiler_params=pltpu.CompilerParams(
            collective_id=0, has_side_effects=True, vmem_limit_bytes=63 * 1024 * 1024
        ),
        cost_estimate=pl.CostEstimate(
            flops=4 * scores * head, bytes_accessed=4 * rows * width, transcendentals=scores
        ),
    )(queries, key_codes, value_codes, key_scales, value_scales, masks)
    return pl.pallas_call(
        functools.partial(place_kernel, pieces),
        out_shape=jax.ShapeDtypeStruct((rows, width), jnp.bfloat16),
        in_specs=[hbm],
        out_specs=hbm,
        scratch_shapes=[dma((pieces,))],
        compiler_params=pltpu.CompilerParams(vmem_limit_bytes=63 * 1024 * 1024),
        cost_estimate=pl.CostEstimate(
            flops=0, bytes_accessed=4 * rows * width, transcendentals=0
        ),
    )(attended)


def solution(mesh):
    both = P(("clip", "sp"), None)
    return jax.shard_map(
        functools.partial(local, mesh.shape["sp"]),
        mesh=mesh,
        in_specs=(both, both, both, both, both, P("clip", None, None)),
        out_specs=both,
        check_vma=False,
    )
```

time: 49.7 us -> 89.9 us (1.81)
  Pallas kernels: 42.8 us -> 89.8 us
  local copies, waits for them, and re-layouts: 6.56 us -> 0 us
    pallas_call x0 -> x1, Pallas kernels: none -> 48.8 us  [local(): pl.pallas_call(functools.partial(place_kernel, pieces), out_shape=jax.Sha...]
    unnamed x12 -> x0, local copies, waits for them, and re-layouts: 6.56 us -> none
    pallas_call x1, Pallas kernels: 42.8 us -> 41 us  [local(): pl.pallas_call(functools.partial(attention_kernel, devices, kv_heads, per...]
where the time goes in v3:
time: 89.9 us; the launch traced here: 89.8 us
  Pallas kernels  89.8 us (100%)
    pallas_call x1, Pallas kernels, local(): pl.pallas_call(functools.partial(place_kernel, pieces), out_shape=jax.Sha...  48.8 us
    pallas_call x1, Pallas kernels, local(): pl.pallas_call(functools.partial(attention_kernel, devices, kv_heads, per...  41 us

profile of v3, /device:TPU:0, one launch (start us, length us, event | category | flops | bytes accessed | tf_op | source)
XLA Modules:
  0.0 89.8 jit_solution(13140144914585940511)
XLA Ops:
  0.0 41.0 %shard_map.64.from_ref = bf16[128,6144]{1,0:T(8,128)(2,1)} custom-call(bf16[128,6144]{1,0:T(8,128)(2,1)} %q_hbm.1, bf16[128,1024]{1,0:T(8,128)(2,1)} %k_hbm.1, bf16[128,1024]{1,0:T(8,128)(2,1)} %v_hbm.1, bf16[1,8]{1,0:T(2,128)(2,1)} %key_scale_hbm.1, bf16[1,8]{1,0:T(2,128)(2,1)} %value_scale_hbm.1, s32[4,4,48]{2,1,0:T(4,128)} %bitcast.1), custom_call_target="tpu_custom_call" | custom-call | flops 1610612736 | bytes 3145728 | tf_op jit(solution)/shard_map/pallas_call | solution.py:310
  41.0 48.8 %shard_map.65 = bf16[128,6144]{1,0:T(8,128)(2,1)} custom-call(bf16[128,6144]{1,0:T(8,128)(2,1)} %shard_map.64.from_ref), custom_call_target="tpu_custom_call" | custom-call | bytes 3145728 | tf_op jit(solution)/shard_map/pallas_call | solution.py:345

commit v4 on v3

--- a/solution.py
+++ b/solution.py
@@ -14,11 +14,11 @@
 
 def attention_kernel(
     devices, kv_heads, per_group, head, rows,
-    q_hbm, k_hbm, v_hbm, key_scale_hbm, value_scale_hbm, masks_hbm, out_hbm,
-    q_ref, q_turned, codes, scales, tops, totals, sums, stage,
+    q_hbm, k_hbm, v_hbm, key_scale_hbm, value_scale_hbm, masks_hbm, out_ref,
+    q_ref, q_turned, codes, scales, tops, totals, sums,
     key_scale_ref, value_scale_ref, masks_ref,
     q_sem, small_sem, own_sem, send_right, send_left, scale_right, scale_left,
-    recv_sem, scale_recv, out_sem,
+    recv_sem, scale_recv,
 ):
     me = lax.axis_index("sp")
     has_left = me > 0
@@ -80,10 +80,6 @@
             device_id_type=MESH,
         )
 
-    def out_copy(g):
-        columns = pl.ds(pl.multiple_of(g * wide, wide), wide)
-        return pltpu.make_async_copy(stage.at[:, columns], out_hbm.at[:, columns], out_sem.at[g])
-
     for copy in small_copies():
         copy.start()
     for g in range(kv_heads):
@@ -133,7 +129,13 @@
 
     ones = jnp.ones((16, rows), jnp.bfloat16)
 
-    def attend(tile, g, first=False):
+    def put(g, r, normed):
+        for o in range(pair):
+            place = pl.ds(pl.multiple_of((g * per_group + r + o) * head, head), head)
+            piece = normed[:, o * rows : (o + 1) * rows]
+            out_ref[:, place] = jnp.transpose(piece).astype(jnp.bfloat16)
+
+    def attend(tile, g, first=False, last=False):
         both = scales[tile].astype(jnp.float32)
         place = lax.broadcasted_iota(jnp.int32, both.shape, 0)
         key_scale = jnp.sum(jnp.where(place == g, both, 0.0), axis=0, keepdims=True)
@@ -174,7 +176,8 @@
                 before = tops[g, :, columns]
                 top = jnp.maximum(before, top)
                 rescale = jnp.exp2(before - top)
-            tops[g, :, columns] = top
+            if not last:
+                tops[g, :, columns] = top
             expo = jnp.exp2(raw * key_scale - (top - bias)).astype(jnp.bfloat16)
             added = jnp.dot(values, expo, preferred_element_type=jnp.float32)
             product = added[:head] * value_scale
@@ -182,16 +185,16 @@
             if not first:
                 product = product + sums[g, :, columns] * rescale
                 total = total + totals[g, :, columns] * rescale
-            sums[g, :, columns] = product
-            totals[g, :, columns] = total
+            if last:
+                put(g, r, product * (1.0 / total))
+            else:
+                sums[g, :, columns] = product
+                totals[g, :, columns] = total
 
     def finish(g):
-        for r in range(per_group):
-            columns = pl.ds(r * rows, rows)
-            place = pl.ds(pl.multiple_of((g * per_group + r) * head, head), head)
-            normed = sums[g, :, columns] * (1.0 / totals[g, :, columns])
-            stage[:, place] = jnp.transpose(normed).astype(jnp.bfloat16)
-        out_copy(g).start()
+        for r in range(0, per_group, pair):
+            columns = pl.ds(r * rows, pair * rows)
+            put(g, r, sums[g, :, columns] * (1.0 / totals[g, :, columns]))
 
     lag = middle.astype(jnp.int32)
 
@@ -202,6 +205,9 @@
         from_right = jnp.logical_and(arrives, right <= devices - 1)
         span = step - lag
         near, far = me - span, me + span
+        between = span > 0
+        if devices % 2 == 0:
+            between = jnp.logical_and(between, span < last_step)
 
         @pl.when(from_left)
         def _():
@@ -240,17 +246,20 @@
             def _():
                 attend(me, g, first=True)
 
-            @pl.when(jnp.logical_and(span > 0, near >= 0))
+            @pl.when(jnp.logical_and(between, near >= 0))
             def _():
                 attend(near, g)
 
-            @pl.when(jnp.logical_and(span > 0, far <= devices - 1))
+            @pl.when(jnp.logical_and(between, far <= devices - 1))
             def _():
                 attend(far, g)
 
             @pl.when(span == last_step)
             def _():
-                finish(g)
+                if devices % 2 == 0:
+                    attend(jnp.where(near >= 0, near, far), g, last=True)
+                else:
+                    finish(g)
 
             return inner
 
@@ -273,26 +282,6 @@
         return carry
 
     lax.fori_loop(0, devices, drain, 0)
-
-    def flush(g, carry):
-        out_copy(g).wait()
-        return carry
-
-    lax.fori_loop(0, kv_heads, flush, 0)
-
-
-def place_kernel(pieces, from_ref, to_ref, sems):
-    rows = from_ref.shape[0] // pieces
-    copies = [
-        pltpu.make_async_copy(
-            from_ref.at[pl.ds(p * rows, rows)], to_ref.at[pl.ds(p * rows, rows)], sems.at[p]
-        )
-        for p in range(pieces)
-    ]
-    for copy in copies:
-        copy.start()
-    for copy in copies:
-        copy.wait()
 
 
 def local(devices, queries, key_codes, value_codes, key_scales, value_scales, masks):
@@ -303,15 +292,14 @@
     head = width // heads
     per_group = heads // kv_heads
     tall = per_group * rows
-    pieces = rows // 16
     hbm = pl.BlockSpec(memory_space=pltpu.HBM)
     dma = pltpu.SemaphoreType.DMA
     scores = heads * rows * rows * devices
-    attended = pl.pallas_call(
+    return pl.pallas_call(
         functools.partial(attention_kernel, devices, kv_heads, per_group, head, rows),
         out_shape=jax.ShapeDtypeStruct((rows, width), jnp.bfloat16),
         in_specs=[hbm] * 6,
-        out_specs=hbm,
+        out_specs=pl.BlockSpec(memory_space=pltpu.VMEM),
         scratch_shapes=[
             pltpu.VMEM((rows, width), jnp.bfloat16),
             pltpu.VMEM((kv_heads, head, tall), jnp.bfloat16),
@@ -320,7 +308,6 @@
             pltpu.VMEM((kv_heads, 1, tall), jnp.float32),
             pltpu.VMEM((kv_heads, 1, tall), jnp.float32),
             pltpu.VMEM((kv_heads, head, tall), jnp.float32),
-            pltpu.VMEM((rows, width), jnp.bfloat16),
             pltpu.VMEM(key_scales.shape, jnp.bfloat16),
             pltpu.VMEM(value_scales.shape, jnp.bfloat16),
             pltpu.SMEM(masks.shape, jnp.int32),
@@ -333,26 +320,19 @@
             dma((devices,)),
             dma((devices, kv_heads)),
             dma((devices,)),
-            dma((kv_heads,)),
         ],
         compiler_params=pltpu.CompilerParams(
-            collective_id=0, has_side_effects=True, vmem_limit_bytes=63 * 1024 * 1024
+            collective_id=0, has_side_effects=True, vmem_limit_bytes=40 * 1024 * 1024
         ),
         cost_estimate=pl.CostEstimate(
             flops=4 * scores * head, bytes_accessed=4 * rows * width, transcendentals=scores
         ),
-    )(queries, key_codes, value_codes, key_scales, value_scales, masks)
-    return pl.pallas_call(
-        functools.partial(place_kernel, pieces),
-        out_shape=jax.ShapeDtypeStruct((rows, width), jnp.bfloat16),
-        in_specs=[hbm],
-        out_specs=hbm,
-        scratch_shapes=[dma((pieces,))],
-        compiler_params=pltpu.CompilerParams(vmem_limit_bytes=63 * 1024 * 1024),
-        cost_estimate=pl.CostEstimate(
-            flops=0, bytes_accessed=4 * rows * width, transcendentals=0
-        ),
-    )(attended)
+    )(
+        *(
+            pltpu.with_memory_space_constraint(operand, pltpu.HBM)
+            for operand in (queries, key_codes, value_codes, key_scales, value_scales, masks)
+        )
+    )
 
 
 def solution(mesh):

time: 89.9 us -> 41.5 us (0.46)
  Pallas kernels: 89.8 us -> 40.2 us
  local copies, waits for them, and re-layouts: 0 us -> 1.15 us
    pallas_call x1 -> x0, Pallas kernels: 48.8 us -> none  [local(): pl.pallas_call(functools.partial(place_kernel, pieces), out_shape=jax.Sha...]
    unnamed x0 -> x1, local copies, waits for them, and re-layouts: none -> 1.15 us
where the time goes in v4:
time: 41.5 us; the launch traced here: 41.4 us
  Pallas kernels  40.2 us (97%)
  local copies, waits for them, and re-layouts  1.15 us (3%)
    pallas_call x1, Pallas kernels, local(): pl.pallas_call(functools.partial(attention_kernel, devices, kv_heads, per...  40.2 us
    unnamed x1, local copies, waits for them, and re-layouts  1.15 us

profile of v4, /device:TPU:0, one launch (start us, length us, event | category | flops | bytes accessed | tf_op | source)
XLA Modules:
  0.0 41.4 jit_solution(11674299378408319514)
XLA Ops:
  0.0 40.2 %shard_map.64 = bf16[128,6144]{1,0:T(8,128)(2,1)S(1)} custom-call(bf16[128,6144]{1,0:T(8,128)(2,1)} %q_hbm.1, bf16[128,1024]{1,0:T(8,128)(2,1)} %k_hbm.1, bf16[128,1024]{1,0:T(8,128)(2,1)} %v_hbm.1, bf16[1,8]{1,0:T(2,128)(2,1)} %key_scale_hbm.1, bf16[1,8]{1,0:T(2,128)(2,1)} %value_scale_hbm.1, s32[4,4,48]{2,1,0:T(4,128)} %bitcast.1), custom_call_target="tpu_custom_call" | custom-call | flops 1610612736 | bytes 3145728 | tf_op jit(solution)/shard_map/pallas_call | solution.py:298
  40.2 1.1 %copy.8 = bf16[128,6144]{1,0:T(8,128)(2,1)} copy(bf16[128,6144]{1,0:T(8,128)(2,1)S(1)} %shard_map.64) | data formatting | bytes 3145728

commit v5 on v4

--- a/solution.py
+++ b/solution.py
@@ -18,7 +18,7 @@
     q_ref, q_turned, codes, scales, tops, totals, sums,
     key_scale_ref, value_scale_ref, masks_ref,
     q_sem, small_sem, own_sem, send_right, send_left, scale_right, scale_left,
-    recv_sem, scale_recv,
+    recv_sem, scale_recv, ready,
 ):
     me = lax.axis_index("sp")
     has_left = me > 0
@@ -31,10 +31,6 @@
 
     barrier = pltpu.get_barrier_semaphore()
 
-    @pl.when(has_left)
-    def _():
-        pl.semaphore_signal(barrier, inc=1, device_id={"sp": me - 1}, device_id_type=MESH)
-
     @pl.when(has_right)
     def _():
         pl.semaphore_signal(barrier, inc=1, device_id={"sp": me + 1}, device_id_type=MESH)
@@ -94,37 +90,44 @@
         picked = jnp.sum(jnp.where(place == other, spread, 0.0), axis=1, keepdims=True)
         return jnp.broadcast_to(picked, (kv_heads, head))
 
+    @pl.when(has_left)
+    def _():
+        pl.semaphore_wait(barrier, 1)
+        pl.semaphore_signal(ready, inc=1, device_id={"sp": me - 1}, device_id_type=MESH)
+
     for copy in small_copies():
         copy.wait()
     scales[me] = jnp.concatenate(
         [column(key_scale_ref), column(value_scale_ref)], axis=0
     ).astype(jnp.bfloat16)
 
-    pl.semaphore_wait(barrier, has_left.astype(jnp.int32) + has_right.astype(jnp.int32))
-
-    @pl.when(has_right)
-    def _():
-        scale_copy(me, me + 1, scale_right).start()
-
     @pl.when(has_left)
     def _():
         scale_copy(me, me - 1, scale_left).start()
 
-    def send_own(g, carry):
+    def send_left_own(g, carry):
         for copy in own_copies(g):
             copy.wait()
 
-        @pl.when(has_right)
-        def _():
+        @pl.when(has_left)
+        def _():
+            code_copy(me, g, me - 1, send_left).start()
+
+        return carry
+
+    lax.fori_loop(0, kv_heads, send_left_own, 0)
+
+    @pl.when(has_right)
+    def _():
+        pl.semaphore_wait(ready, 1)
+        scale_copy(me, me + 1, scale_right).start()
+
+        def send_right_own(g, carry):
             code_copy(me, g, me + 1, send_right).start()
-
-        @pl.when(has_left)
-        def _():
-            code_copy(me, g, me - 1, send_left).start()
-
-        return carry
-
-    lax.fori_loop(0, kv_heads, send_own, 0)
+            return carry
+
+        lax.fori_loop(0, kv_heads, send_right_own, 0)
+
     q_copy().wait()
 
     ones = jnp.ones((16, rows), jnp.bfloat16)
@@ -320,6 +323,7 @@
             dma((devices,)),
             dma((devices, kv_heads)),
             dma((devices,)),
+            pltpu.SemaphoreType.REGULAR,
         ],
         compiler_params=pltpu.CompilerParams(
             collective_id=0, has_side_effects=True, vmem_limit_bytes=40 * 1024 * 1024

time: 41.5 us -> 41.2 us (level)
  no operation moved by 1% of the time
where the time goes in v5:
time: 41.2 us; the launch traced here: 41.1 us
  Pallas kernels  39.9 us (97%)
  local copies, waits for them, and re-layouts  1.15 us (3%)
    pallas_call x1, Pallas kernels, local(): pl.pallas_call(functools.partial(attention_kernel, devices, kv_heads, per...  39.9 us
    unnamed x1, local copies, waits for them, and re-layouts  1.15 us

profile of v5, /device:TPU:0, one launch (start us, length us, event | category | flops | bytes accessed | tf_op | source)
XLA Modules:
  0.0 41.1 jit_solution(18204808381509841397)
XLA Ops:
  0.0 39.9 %shard_map.64 = bf16[128,6144]{1,0:T(8,128)(2,1)S(1)} custom-call(bf16[128,6144]{1,0:T(8,128)(2,1)} %q_hbm.1, bf16[128,1024]{1,0:T(8,128)(2,1)} %k_hbm.1, bf16[128,1024]{1,0:T(8,128)(2,1)} %v_hbm.1, bf16[1,8]{1,0:T(2,128)(2,1)} %key_scale_hbm.1, bf16[1,8]{1,0:T(2,128)(2,1)} %value_scale_hbm.1, s32[4,4,48]{2,1,0:T(4,128)} %bitcast.1), custom_call_target="tpu_custom_call" | custom-call | flops 1610612736 | bytes 3145728 | tf_op jit(solution)/shard_map/pallas_call | solution.py:301
  39.9 1.1 %copy.8 = bf16[128,6144]{1,0:T(8,128)(2,1)} copy(bf16[128,6144]{1,0:T(8,128)(2,1)S(1)} %shard_map.64) | data formatting | bytes 3145728

commit v6 on v5

--- a/solution.py
+++ b/solution.py
@@ -95,6 +95,18 @@
         pl.semaphore_wait(barrier, 1)
         pl.semaphore_signal(ready, inc=1, device_id={"sp": me - 1}, device_id_type=MESH)
 
+    def send_left_own(g, carry):
+        for copy in own_copies(g):
+            copy.wait()
+
+        @pl.when(has_left)
+        def _():
+            code_copy(me, g, me - 1, send_left).start()
+
+        return carry
+
+    lax.fori_loop(0, 1, send_left_own, 0)
+
     for copy in small_copies():
         copy.wait()
     scales[me] = jnp.concatenate(
@@ -105,17 +117,7 @@
     def _():
         scale_copy(me, me - 1, scale_left).start()
 
-    def send_left_own(g, carry):
-        for copy in own_copies(g):
-            copy.wait()
-
-        @pl.when(has_left)
-        def _():
-            code_copy(me, g, me - 1, send_left).start()
-
-        return carry
-
-    lax.fori_loop(0, kv_heads, send_left_own, 0)
+    lax.fori_loop(1, kv_heads, send_left_own, 0)
 
     @pl.when(has_right)
     def _():

time: 41.2 us -> 41 us (level)
  no operation moved by 1% of the time
where the time goes in v6:
time: 41 us; the launch traced here: 40.9 us
  Pallas kernels  39.7 us (97%)
  local copies, waits for them, and re-layouts  1.15 us (3%)
    pallas_call x1, Pallas kernels, local(): pl.pallas_call(functools.partial(attention_kernel, devices, kv_heads, per...  39.7 us
    unnamed x1, local copies, waits for them, and re-layouts  1.15 us

profile of v6, /device:TPU:0, one launch (start us, length us, event | category | flops | bytes accessed | tf_op | source)
XLA Modules:
  0.0 40.9 jit_solution(5177098445659295178)
XLA Ops:
  0.0 39.7 %shard_map.64 = bf16[128,6144]{1,0:T(8,128)(2,1)S(1)} custom-call(bf16[128,6144]{1,0:T(8,128)(2,1)} %q_hbm.1, bf16[128,1024]{1,0:T(8,128)(2,1)} %k_hbm.1, bf16[128,1024]{1,0:T(8,128)(2,1)} %v_hbm.1, bf16[1,8]{1,0:T(2,128)(2,1)} %key_scale_hbm.1, bf16[1,8]{1,0:T(2,128)(2,1)} %value_scale_hbm.1, s32[4,4,48]{2,1,0:T(4,128)} %bitcast.1), custom_call_target="tpu_custom_call" | custom-call | flops 1610612736 | bytes 3145728 | tf_op jit(solution)/shard_map/pallas_call | solution.py:303
  39.7 1.1 %copy.8 = bf16[128,6144]{1,0:T(8,128)(2,1)} copy(bf16[128,6144]{1,0:T(8,128)(2,1)S(1)} %shard_map.64) | data formatting | bytes 3145728
